TPU v7x, 128 devices: a whole 4x4x4 slice. The times are simulated.
128 devices in a mesh: expert: 16 (over x, z), dp: 8 (over y, core).
Axes of the slice: x: 4, y: 4, z: 4, core: 2. Of those that a mesh axis runs over, the one named last changes fastest.
Arguments:
- tokens: bfloat16 [1024, 7168], P(('expert', 'dp')), may hold values from -6 to 6
- routes: int32 [1024, 8], P(('expert', 'dp')), may hold values from 0 to 15, all different within a row; in each aligned block of 64 rows (0 to 63, 64 to 127, ...) at most 48 rows name the same one
- gates: bfloat16 [1024, 8], P(('expert', 'dp')), may hold values from 0.099609375 to 1
- swapped: int32 [8], replicated, may hold values from 0 to 1, as said below
- gate_weight: bfloat16 [16, 7168, 2048], P('expert', None, 'dp'), may hold values from -6 to 6
- up_weight: bfloat16 [16, 7168, 2048], P('expert', None, 'dp'), may hold values from -6 to 6
- down_weight: bfloat16 [16, 2048, 7168], P('expert', 'dp'), may hold values from -6 to 6
Outputs:
- mixed: bfloat16 [1024, 7168], P(('expert', 'dp'))
- moved_gate: bfloat16 [16, 7168, 2048], P('expert', None, 'dp')
- moved_up: bfloat16 [16, 7168, 2048], P('expert', None, 'dp')
- moved_down: bfloat16 [16, 2048, 7168], P('expert', 'dp')
Inputs may be any that keep to these rules, and one draw needn't show every extreme that they name: `routes`: each row names 8 different experts. In each aligned block of 64 rows (the tokens held by the 8 dp devices of one index along `expert` (an aligned block of 64 rows)) no expert is named by more than 48 rows, a bound that some block reaches. `swapped`: pair 0 always exchanges its slabs; each other pair does so independently with probability one half.
All inputs are finite; a program needn't handle non-finite values.
Results may differ from a plain program's by a relative error of at most 0.014.
Values may be sent and summed in bfloat16 or wider, within the bound.
A program may use at most 192 MiB of HBM per device.

v0:
```python
import jax
import jax.numpy as jnp
from jax import lax
from jax.sharding import PartitionSpec as P

D = 7168
FF = 2048


def partner(value, axis, distance):
    mask = 2**distance
    pairs = [(source, source ^ mask) for source in range(lax.axis_size(axis))]
    return lax.ppermute(value, axis, pairs)


def expert_part(rows, w_gate, w_up, w_down):
    pre_gate = jnp.dot(rows, w_gate, preferred_element_type=jnp.float32) * D ** (-0.5)
    pre_up = jnp.dot(rows, w_up, preferred_element_type=jnp.float32) * D ** (-0.5)
    hidden = (jax.nn.silu(pre_gate) * pre_up).astype(jnp.bfloat16)
    return (jnp.dot(hidden, w_down, preferred_element_type=jnp.float32) * FF ** (-0.5)).astype(
        jnp.bfloat16
    )


def slot_positions(flat_dest, count):
    hits = (flat_dest[:, None] == jnp.arange(count, dtype=jnp.int32)[None, :]).astype(jnp.int32)
    before = jnp.cumsum(hits, axis=0) - hits
    return jnp.sum(before * hits, axis=1)


def on_device(tokens, routes, gates, swapped, gate_weight, up_weight, down_weight):
    count = lax.axis_size("expert")
    half = count // 2
    mine = lax.axis_index("expert")
    model = tokens.shape[1]
    top = routes.shape[1]
    received = partner((gate_weight, up_weight, down_weight), "expert", count.bit_length() - 2)
    flag = swapped[mine % half] == 1
    moved_gate = jnp.where(flag, received[0], gate_weight)
    moved_up = jnp.where(flag, received[1], up_weight)
    moved_down = jnp.where(flag, received[2], down_weight)
    w_gate, w_up, w_down = (moved_gate[0], moved_up[0], moved_down[0])
    pair_flag = swapped[routes % half] == 1
    dest = jnp.where(pair_flag, (routes + half) % count, routes)
    group_tok, group_dest, group_gates = (
        lax.all_gather(tokens, "dp", axis=0, tiled=True),
        lax.all_gather(dest, "dp", axis=0, tiled=True),
        lax.all_gather(gates, "dp", axis=0, tiled=True),
    )
    group = group_tok.shape[0]
    cap = group * top * 3 // (2 * count)
    flat_dest = group_dest.reshape(-1)
    position = slot_positions(flat_dest, count)
    target = flat_dest * cap + position
    entry = jnp.arange(group * top, dtype=jnp.int32)
    table = jnp.full((count * cap,), -1, jnp.int32).at[target].set(entry // top)
    safe = jnp.maximum(table, 0)
    send = jnp.where((table >= 0)[:, None], group_tok[safe], jnp.zeros((), jnp.bfloat16)).reshape(
        count, cap, model
    )
    block = lax.all_to_all(send, "expert", split_axis=0, concat_axis=0, tiled=True)
    flat = block.reshape(-1, model)
    partials = expert_part(flat, w_gate, w_up, w_down).reshape(block.shape)
    back = lax.all_to_all(partials, "expert", split_axis=0, concat_axis=0, tiled=True)
    picked = back.reshape(count * cap, model)[target].reshape(group, top, model)
    weighted = jnp.sum(
        picked.astype(jnp.float32) * group_gates.astype(jnp.float32)[:, :, None], axis=1
    )
    mixed = lax.psum_scatter(weighted, "dp", scatter_dimension=0, tiled=True).astype(jnp.bfloat16)
    return (mixed, moved_gate, moved_up, moved_down)


def solution(mesh):
    in_specs = (
        P(("expert", "dp"), None),
        P(("expert", "dp"), None),
        P(("expert", "dp"), None),
        P(),
        P("expert", None, "dp"),
        P("expert", None, "dp"),
        P("expert", "dp", None),
    )
    out_specs = (
        P(("expert", "dp"), None),
        P("expert", None, "dp"),
        P("expert", None, "dp"),
        P("expert", "dp", None),
    )
    return jax.shard_map(
        on_device, mesh=mesh, in_specs=in_specs, out_specs=out_specs, check_vma=False
    )
```

profile of v0, /device:TPU:0, one launch (start us, length us, event | category | flops | bytes accessed | tf_op | source)
XLA Modules:
  0.0 797.3 jit_solution(15638281331232877045)
XLA Ops:
  7.2 0.8 compare_select_fusion.1
  8.0 1.4 gather_fusion
  9.6 13.4 %all_gather.9 = s32[64,8]{1,0:T(8,128)S(1)} all-gather(s32[8,8]{1,0:T(8,128)S(1)} %fusion.24), channel_id=1, replica_groups=mesh['expert'=16,'dp'=8] {'dp'}, dimensions={0}, use_global_device_ids=true | all-gather | bytes 2304 | tf_op jit(solution)/shard_map/all_gather | solution.py:47
  23.0 0.1 eq.48
  23.2 1.2 reduce-window.6
  24.4 0.2 slice_reduce_fusion
  24.6 0.1 mul.48
  24.7 0.1 fusion.20
  24.8 2.4 scatter_custom_fusion
  27.3 13.5 %all_gather.10 = bf16[64,7168]{1,0:T(8,128)(2,1)S(1)} all-gather(bf16[8,7168]{1,0:T(8,128)(2,1)S(1)} %copy-done.3), channel_id=1, replica_groups=mesh['expert'=16,'dp'=8] {'dp'}, dimensions={0}, use_global_device_ids=true | all-gather | bytes 1032192 | tf_op jit(solution)/shard_map/all_gather | solution.py:46
  41.0 9.5 %gather_fusion.1 = bf16[768,7168]{1,0:T(8,128)(2,1)} fusion(bf16[64,7168]{1,0:T(8,128)(2,1)S(1)} %all_gather.10, s32[1024]{0:T(1024)S(1)} %pad_clamp_fusion.1), kind=kCustom, calls=%fused_computation.1 | custom fusion | bytes 22023168 | tf_op jit(solution)/shard_map/gather | solution.py:58
  50.4 9.8 %broadcast_select_fusion = bf16[16,48,7168]{2,1,0:T(8,128)(2,1)} fusion(bf16[16,48,7168]{2,1,0:T(8,128)(2,1)} %bitcast.48, pred[16,48]{1,0:T(8,128)(4,1)S(1)} %broadcast_in_dim.30), kind=kLoop, calls=%fused_computation.7 | loop fusion | flops 5505024 | bytes 22020864 | tf_op jit(solution)/shard_map/jit(_where)/select_n | solution.py:58
  60.3 8.1 %all-to-all-start = ((bf16[16,48,7168]{2,1,0:T(8,128)(2,1)}), bf16[16,48,7168]{2,1,0:T(8,128)(2,1)}, u32[]{:S(2)}, u32[]{:S(2)}) async-start(bf16[16,48,7168]{2,1,0:T(8,128)(2,1)} %broadcast_select_fusion), calls=%async_computation | async-start | bytes 22020096 | tf_op jit(solution)/shard_map/all_to_all | solution.py:61
  68.3 3.4 collective-permute-start
  71.7 0.2 collective-permute-start.1
  71.9 3.3 collective-permute-start.2
  75.2 0.6 dynamic_slice.3
  76.5 260.4 %collective-permute-done = bf16[1,7168,256]{2,1,0:T(8,128)(2,1)} collective-permute-done((bf16[1,7168,256]{2,1,0:T(8,128)(2,1)}, bf16[1,7168,256]{2,1,0:T(8,128)(2,1)}, u32[]{:S(2)}, u32[]{:S(2)}) %collective-permute-start) | collective-permute-done | bytes 3670048 | tf_op jit(solution)/shard_map/ppermute | solution.py:13
  336.8 4.4 broadcast_select_fusion.3
  341.2 74.2 %collective-permute-done.1 = bf16[1,7168,256]{2,1,0:T(8,128)(2,1)} collective-permute-done((bf16[1,7168,256]{2,1,0:T(8,128)(2,1)}, bf16[1,7168,256]{2,1,0:T(8,128)(2,1)}, u32[]{:S(2)}, u32[]{:S(2)}) %collective-permute-start.1) | collective-permute-done | bytes 3670048 | tf_op jit(solution)/shard_map/ppermute | solution.py:13
  415.5 4.3 broadcast_select_fusion.2
  419.7 73.8 %collective-permute-done.2 = bf16[1,256,7168]{2,1,0:T(8,128)(2,1)} collective-permute-done((bf16[1,256,7168]{2,1,0:T(8,128)(2,1)}, bf16[1,256,7168]{2,1,0:T(8,128)(2,1)}, u32[]{:S(2)}, u32[]{:S(2)}) %collective-permute-start.2) | collective-permute-done | bytes 3670048 | tf_op jit(solution)/shard_map/ppermute | solution.py:13
  493.6 4.3 broadcast_select_fusion.1
  497.8 6.9 fusion.6
  504.7 18.9 %multiply_convert_fusion = bf16[768,7168]{1,0:T(8,128)(2,1)} fusion(bf16[1,256,7168]{2,1,0:T(8,128)(2,1)} %broadcast_select_fusion.1, f32[768,256]{1,0:T(8,128)S(1)} %fusion.6, bf16[768,7168]{1,0:T(8,128)(2,1)} %bitcast.4, bf16[1,7168,256]{2,1,0:T(8,128)(2,1)} %broadcast_select_fusion.2), kind=kOutput, calls=%fused_computation.4 | convolution fusion | flops 5649530880 | bytes 30146560 | tf_op jit(solution)/shard_map/dot_general | solution.py:20
  523.6 6.6 all-to-all-start.1
  530.2 11.2 %all_gather.11 = bf16[64,8]{1,0:T(8,128)(2,1)S(1)} all-gather(bf16[8,8]{1,0:T(8,128)(2,1)S(1)} %copy-done.5), channel_id=1, replica_groups=mesh['expert'=16,'dp'=8] {'dp'}, dimensions={0}, use_global_device_ids=true | all-gather | bytes 1152 | tf_op jit(solution)/shard_map/all_gather | solution.py:48
  541.5 181.1 %all-to-all-done.1 = bf16[16,48,7168]{2,1,0:T(8,128)(2,1)} async-done(((bf16[16,48,7168]{2,1,0:T(8,128)(2,1)}), bf16[16,48,7168]{2,1,0:T(8,128)(2,1)}, u32[]{:S(2)}, u32[]{:S(2)}) %all-to-all-start.1) | async-done | bytes 11010080 | tf_op jit(solution)/shard_map/all_to_all | solution.py:64
  722.6 19.5 %gather_fusion.2 = bf16[512,7168]{1,0:T(8,128)(2,1)} fusion(bf16[768,7168]{1,0:T(8,128)(2,1)} %bitcast.10, s32[1024]{0:T(1024)S(1)} %pad_clamp_fusion), kind=kCustom, calls=%fused_computation.2 | custom fusion | bytes 14682112 | tf_op jit(solution)/shard_map/gather | solution.py:65
  742.1 10.1 %fusion = f32[64,7168]{1,0:T(8,128)} fusion(bf16[512,7168]{1,0:T(8,128)(2,1)} %gather_fusion.2, f32[64,8]{1,0:T(8,128)S(1)} %convert_element_type.31), kind=kLoop, calls=%fused_computation.6 | loop fusion | flops 10551296 | bytes 9177088 | tf_op jit(solution)/shard_map/reduce_sum | solution.py:66
  752.2 36.6 %reduce-scatter.2.cloned.1.call-done = f32[8,7168]{1,0:T(8,128)} async-done(((f32[64,7168]{1,0:T(8,128)}), f32[8,7168]{1,0:T(8,128)}) %reduce-scatter.2.cloned.1.call-update) | async-done | bytes 229392 | tf_op jit(solution)/shard_map/reduce_scatter | solution.py:69
  788.9 1.6 convert_element_type.32
  (33 shorter events, 0.5 us)
Async XLA Ops:
  7.2 2.4 copy-start.4
  7.2 20.2 %copy-start.3 = (bf16[8,7168]{1,0:T(8,128)(2,1)S(1)}, bf16[8,7168]{1,0:T(8,128)(2,1)}, u32[]{:S(2)}) copy-start(bf16[8,7168]{1,0:T(8,128)(2,1)} %param.7) | copy-start | bytes 344068
  60.2 15.0 %copy-start = (s32[8]{0:T(128)S(1)}, s32[8]{0:T(128)}, u32[]{:S(2)}) copy-start(s32[8]{0:T(128)} %param.10) | copy-start | bytes 100
  60.3 437.6 %all-to-all-start = ((bf16[16,48,7168]{2,1,0:T(8,128)(2,1)}), bf16[16,48,7168]{2,1,0:T(8,128)(2,1)}, u32[]{:S(2)}, u32[]{:S(2)}) async-start(bf16[16,48,7168]{2,1,0:T(8,128)(2,1)} %broadcast_select_fusion), calls=%async_computation | async-start | bytes 22020096 | tf_op jit(solution)/shard_map/all_to_all | solution.py:61
  68.3 268.5 %collective-permute-start = (bf16[1,7168,256]{2,1,0:T(8,128)(2,1)}, bf16[1,7168,256]{2,1,0:T(8,128)(2,1)}, u32[]{:S(2)}, u32[]{:S(2)}) collective-permute-start(bf16[1,7168,256]{2,1,0:T(8,128)(2,1)} %param.11), channel_id=1, source_target_pairs={{0,64},{8,72},{16,80},{24,88},{32,96},{40,104},{48,112},{56,120},{... | collective-permute-start | bytes 11010056 | tf_op jit(solution)/shard_map/ppermute | solution.py:13
  71.7 343.8 %collective-permute-start.1 = (bf16[1,7168,256]{2,1,0:T(8,128)(2,1)}, bf16[1,7168,256]{2,1,0:T(8,128)(2,1)}, u32[]{:S(2)}, u32[]{:S(2)}) collective-permute-start(bf16[1,7168,256]{2,1,0:T(8,128)(2,1)} %param.12), channel_id=1, source_target_pairs={{0,64},{8,72},{16,80},{24,88},{32,96},{40,104},{48,112},{56,120},{... | collective-permute-start | bytes 11010056 | tf_op jit(solution)/shard_map/ppermute | solution.py:13
  71.9 421.6 %collective-permute-start.2 = (bf16[1,256,7168]{2,1,0:T(8,128)(2,1)}, bf16[1,256,7168]{2,1,0:T(8,128)(2,1)}, u32[]{:S(2)}, u32[]{:S(2)}) collective-permute-start(bf16[1,256,7168]{2,1,0:T(8,128)(2,1)} %param.13), channel_id=1, source_target_pairs={{0,64},{8,72},{16,80},{24,88},{32,96},{40,104},{48,112},{56,120},{... | collective-permute-start | bytes 11010056 | tf_op jit(solution)/shard_map/ppermute | solution.py:13
  336.8 78.6 %copy-start.1 = (bf16[1,7168,256]{2,1,0:T(8,128)(2,1)S(1)}, bf16[1,7168,256]{2,1,0:T(8,128)(2,1)}, u32[]{:S(2)}) copy-start(bf16[1,7168,256]{2,1,0:T(8,128)(2,1)} %param.12) | copy-start | bytes 11010052
  341.2 152.3 %copy-start.2 = (bf16[1,256,7168]{2,1,0:T(8,128)(2,1)S(1)}, bf16[1,256,7168]{2,1,0:T(8,128)(2,1)}, u32[]{:S(2)}) copy-start(bf16[1,256,7168]{2,1,0:T(8,128)(2,1)} %param.13) | copy-start | bytes 11010052
  523.6 6.6 copy-start.5
  523.6 199.0 %all-to-all-start.1 = ((bf16[16,48,7168]{2,1,0:T(8,128)(2,1)}), bf16[16,48,7168]{2,1,0:T(8,128)(2,1)}, u32[]{:S(2)}, u32[]{:S(2)}) async-start(bf16[16,48,7168]{2,1,0:T(8,128)(2,1)} %bitcast.49), calls=%async_computation.1 | async-start | bytes 22020096 | tf_op jit(solution)/shard_map/all_to_all | solution.py:64
  530.2 258.7 %reduce-scatter.2.cloned.1.call-start = ((), (), s32[]{:S(2)}) async-start(), calls=%async_computation.3 | async-start | bytes 2064384 | tf_op jit(solution)/shard_map/reduce_scatter | solution.py:69
Sparse Core Ops, SparseCore 0:
  752.4 36.4 reduce-scatter.1
where the time goes:
time: 799 us; the launch traced here: 797 us
  waiting for transfers between devices  626 us (78%)
  blocking collectives  38.2 us (5%)
  other arithmetic  36.5 us (5%)
  local copies, waits for them, and re-layouts  34.2 us (4%)
  matrix products  25.8 us (3%)
  starting transfers between devices  21.6 us (3%)
  between operations  14.8 us (2%)
    ppermute x3, waiting for transfers between devices, partner(): return lax.ppermute(value, axis, pairs)  408 us
    all_to_all x1, waiting for transfers between devices, on_device(): lax.all_to_all(partials, 'expert', split_axis=0, concat_axis=0, tiled=True)  181 us
    reduce_scatter x1, waiting for transfers between devices, on_device(): lax.psum_scatter(weighted, 'dp', scatter_dimension=0, tiled=True)  36.6 us
    gather x1, local copies, waits for them, and re-layouts, on_device(): picked = back.reshape(count * cap, model)[target].reshape(group, top, model)  19.5 us
    dot_general x1, matrix products, expert_part(): jnp.dot(hidden, w_down, preferred_element_type=jnp.float32) * FF ** (-0.5)  18.9 us
  transfers between devices with their start and end apart: 6, of which 5 were waited for; matrix products, arithmetic and copies ran while one was open for 2% of the time, Pallas kernels for 0%

commit v1 on v0

v1 whole, which is shorter than its diff:
```python
import functools

import jax
import jax.numpy as jnp
from jax import lax
from jax.experimental import pallas as pl
from jax.experimental.pallas import tpu as pltpu
from jax.sharding import PartitionSpec as P

D = 7168
FF = 2048
EXPERTS = 16
Q = D // 4
EXT = 128
W0 = Q + EXT
BF = jnp.bfloat16
F32 = jnp.float32
MESH = pl.DeviceIdType.MESH


def moe_kernel(
    tok, gw, uw, dw,
    out, rg, ru, rd,
    x0, x1, o0, o1, wg, wu, wd,
    mine0, mine1, send0, send1, core0, core1,
    r1a, r1b, s2a, s2b, r2a, r2b, s3a, s3b, r3a, r3b,
    half_in, half_out, last_in,
    wsem, swap_s, swap_r, core_s, core_r, ag_s, ag_r, fw_s, fw_r, pc_s, pc_r, rs_s, rs_r,
):
    e = lax.axis_index("expert")
    d = lax.axis_index("dp")
    x, z = e // 4, lax.rem(e, 4)
    y, c = d // 2, lax.rem(d, 2)

    def shift(value, by):
        return lax.rem(value + by, 4)

    def device(px, pz, py, pc):
        return (px * 4 + pz, py * 2 + pc)

    other = device(x, z, y, 1 - c)
    along = {
        "x": lambda i: device(shift(x, i), z, y, c),
        "z": lambda i: device(x, shift(z, i), y, c),
        "y": lambda i: device(x, z, shift(y, i), c),
    }

    def remote(src, dst, ss, rs, dev):
        return pltpu.make_async_remote_copy(
            src_ref=src, dst_ref=dst, send_sem=ss, recv_sem=rs,
            device_id=dev, device_id_type=MESH,
        )

    loads = [
        pltpu.make_async_copy(gw.at[0], wg, wsem.at[0]),
        pltpu.make_async_copy(uw.at[0], wu, wsem.at[1]),
        pltpu.make_async_copy(dw.at[0], wd, wsem.at[2]),
    ]
    for cp in loads:
        cp.start()

    barrier = pltpu.get_barrier_semaphore()
    peers = [other] + [along[a](i) for a in "xzy" for i in (1, 2, 3)]
    for dev in peers:
        pl.semaphore_signal(barrier, inc=1, device_id=dev, device_id_type=MESH)
    pl.semaphore_wait(barrier, len(peers))

    first = remote(tok.at[1 - c], half_in, core_s.at[0], core_r.at[0], other)
    first.start()

    first.wait()
    own = tok[c]
    got = half_in[...]
    block = jnp.where(
        c == 0, jnp.concatenate([own, got], axis=0), jnp.concatenate([got, own], axis=0)
    ).astype(BF)
    rows16 = pl.ds(pl.multiple_of(x * 16, 16), 16)
    x0[y, z, rows16, 0:Q] = block[:, 0:Q]
    x0[y, z, rows16, Q:W0] = block[:, 2 * Q : 2 * Q + EXT]
    x1[y, z, rows16, :] = block[:, Q : 2 * Q]

    sent = []

    def gather(stream, stage, i, buf, view, axis):
        cp = remote(
            buf.at[view], buf.at[view], ag_s.at[stream, stage, i - 1], ag_r.at[stream, stage, i - 1],
            along[axis](i),
        )
        cp.start()
        sent.append(cp)

    def landed(stream, stage, i, buf, view):
        remote(
            buf.at[view], buf.at[view], ag_s.at[stream, stage, i - 1], ag_r.at[stream, stage, i - 1], other
        ).wait_recv()

    for i in (1, 2, 3):
        gather(0, 0, i, x0, (y, z, rows16), "x")
        gather(1, 0, i, x1, (y, z, rows16), "x")

    swaps = [
        remote(src.at[0], dst.at[0], swap_s.at[k], swap_r.at[k], along["x"](2))
        for k, (src, dst) in enumerate(((gw, rg), (uw, ru), (dw, rd)))
    ]
    for cp in swaps:
        cp.start()

    for i in (1, 2, 3):
        from16 = pl.ds(pl.multiple_of(shift(x, 4 - i) * 16, 16), 16)
        landed(0, 0, i, x0, (y, z, from16))
        landed(1, 0, i, x1, (y, z, from16))
    for i in (1, 2, 3):
        gather(0, 1, i, x0, (y, z), "z")
        gather(1, 1, i, x1, (y, z), "y")
    for i in (1, 2, 3):
        landed(0, 1, i, x0, (y, shift(z, 4 - i)))
        landed(1, 1, i, x1, (shift(y, 4 - i), z))
    every = slice(None)
    for i in (1, 2, 3):
        gather(0, 2, i, x0, (y,), "y")
        gather(1, 2, i, x1, (every, z), "z")

    forwards = []

    def forward(stream, i, view):
        src, dst = ((x0, o0), (x1, o1))[stream]
        cp = remote(src.at[view], dst.at[view], fw_s.at[stream, i], fw_r.at[stream, i], other)
        cp.start()
        forwards.append(cp)

    forward(0, 0, (y,))
    forward(1, 0, (every, z))
    for i in (1, 2, 3):
        view0, view1 = (shift(y, 4 - i),), (every, shift(z, 4 - i))
        landed(0, 2, i, x0, view0)
        forward(0, i, view0)
        landed(1, 2, i, x1, view1)
        forward(1, i, view1)
    for cp in forwards:
        cp.wait()
    for cp in sent:
        cp.wait_send()
    for cp in loads:
        cp.wait()

    lane = lax.broadcasted_iota(jnp.int32, (128, EXT), 1)
    lo = pl.multiple_of(c * 2 * Q, 2 * Q)
    hi = pl.multiple_of((1 - c) * 2 * Q, 2 * Q)

    def rows_of(ref, a, b):
        return ref[a, pl.ds(b * 2, 2)].reshape(128, ref.shape[-1])

    def turn(t, carry):
        a, b = t // 2, lax.rem(t, 2)
        full = rows_of(x0, a, b)
        parts = (
            (full[:, 0:Q], lo),
            (rows_of(x1, a, b), lo + Q),
            (rows_of(o0, a, b)[:, 0:Q], hi),
            (rows_of(o1, a, b), hi + Q),
        )
        gate = jnp.zeros((128, 256), F32)
        up = jnp.zeros((128, 256), F32)
        for part, start in parts:
            at = pl.ds(pl.multiple_of(start, Q), Q)
            gate += jnp.dot(part, wg[at, :], preferred_element_type=F32)
            up += jnp.dot(part, wu[at, :], preferred_element_type=F32)
        gate = gate * D ** (-0.5)
        up = up * D ** (-0.5)
        hidden = (gate / (1.0 + jnp.exp(-gate)) * up).astype(BF)
        weight = jnp.sum(
            jnp.where(lane == e, full[:, Q:W0].astype(F32), 0.0), axis=1, keepdims=True
        ) * FF ** (-0.5)
        for dst, start in ((send0, hi), (send1, hi + Q), (mine0, lo), (mine1, lo + Q)):
            at = pl.ds(pl.multiple_of(start, Q), Q)
            value = jnp.dot(hidden, wd[:, at], preferred_element_type=F32) * weight
            dst[a, pl.ds(b * 2, 2)] = value.astype(BF).reshape(2, 64, Q)
        return carry

    def part_copy(stream, a):
        src, dst = ((send0, core0), (send1, core1))[stream]
        return remote(src.at[a], dst.at[a], pc_s.at[stream, a], pc_r.at[stream, a], other)

    def quarter(a, carry):
        lax.fori_loop(2 * a, 2 * a + 2, turn, 0)
        part_copy(0, a).start()
        part_copy(1, a).start()
        return carry

    lax.fori_loop(0, 4, quarter, 0)

    def add_cores(a, carry):
        part_copy(0, a).wait()
        part_copy(1, a).wait()
        for own_ref, got_ref in ((mine0, core0), (mine1, core1)):
            for b in range(4):
                own_ref[a, b] = (own_ref[a, b].astype(F32) + got_ref[a, b].astype(F32)).astype(BF)
        return carry

    lax.fori_loop(0, 4, add_cores, 0)

    out_copies = []

    def scatter(stream, stage, i, src, dst, axis):
        cp = remote(src, dst, rs_s.at[stream, stage, i - 1], rs_r.at[stream, stage, i - 1], along[axis](i))
        cp.start()
        out_copies.append(cp)
        return cp

    def total(own_value, got_ref, at=()):
        value = own_value.astype(F32)
        for i in range(3):
            value += got_ref[(i,) + at].astype(F32)
        return value

    stage = []
    for i in (1, 2, 3):
        stage.append(scatter(0, 0, i, mine0.at[shift(y, i)], r1a.at[i - 1], "y"))
        stage.append(scatter(1, 0, i, mine1.at[:, shift(z, i)], r1b.at[i - 1], "z"))
    for cp in stage:
        cp.wait_recv()
    for b in range(4):
        s2a[b] = total(mine0[y, b], r1a, (b,)).astype(BF)
        s2b[b] = total(mine1[b, z], r1b, (b,)).astype(BF)
    stage = []
    for i in (1, 2, 3):
        stage.append(scatter(0, 1, i, s2a.at[shift(z, i)], r2a.at[i - 1], "z"))
        stage.append(scatter(1, 1, i, s2b.at[shift(y, i)], r2b.at[i - 1], "y"))
    for cp in stage:
        cp.wait_recv()
    s3a[...] = total(s2a[z], r2a).astype(BF)
    s3b[...] = total(s2b[y], r2b).astype(BF)
    stage = []
    for i in (1, 2, 3):
        to16 = pl.ds(pl.multiple_of(shift(x, i) * 16, 16), 16)
        stage.append(scatter(0, 2, i, s3a.at[to16], r3a.at[i - 1], "x"))
        stage.append(scatter(1, 2, i, s3b.at[to16], r3b.at[i - 1], "x"))
    for cp in stage:
        cp.wait_recv()
    sum_a = total(s3a[rows16, :], r3a)
    sum_b = total(s3b[rows16, :], r3b)
    keep_a = jnp.where(c == 0, sum_a[0:8], sum_a[8:16])
    keep_b = jnp.where(c == 0, sum_b[0:8], sum_b[8:16])
    half_out[:, 0:Q] = jnp.where(c == 0, sum_a[8:16], sum_a[0:8])
    half_out[:, Q : 2 * Q] = jnp.where(c == 0, sum_b[8:16], sum_b[0:8])
    last = remote(half_out, last_in, core_s.at[1], core_r.at[1], other)
    last.start()
    last.wait()
    kept = jnp.concatenate([keep_a, keep_b], axis=1)
    given = last_in[...]
    out[:, 0 : 2 * Q] = jnp.where(c == 0, kept, given).astype(BF)
    out[:, 2 * Q :] = jnp.where(c == 0, given, kept).astype(BF)

    for cp in out_copies:
        cp.wait_send()
    for cp in swaps:
        cp.wait()


def moe(tok, gate_weight, up_weight, down_weight):
    vm = lambda *shape: pltpu.VMEM(shape, BF)
    dma = lambda *shape: pltpu.SemaphoreType.DMA(shape)
    any_spec = pl.BlockSpec(memory_space=pl.ANY)
    vmem_spec = pl.BlockSpec(memory_space=pltpu.VMEM)
    like = lambda a: jax.ShapeDtypeStruct(a.shape, a.dtype)
    return pl.pallas_call(
        moe_kernel,
        out_shape=(
            jax.ShapeDtypeStruct((8, D), BF),
            like(gate_weight), like(up_weight), like(down_weight),
        ),
        in_specs=[vmem_spec, any_spec, any_spec, any_spec],
        out_specs=(vmem_spec, any_spec, any_spec, any_spec),
        scratch_shapes=[
            vm(4, 4, 64, W0), vm(4, 4, 64, Q), vm(4, 4, 64, W0), vm(4, 4, 64, Q),
            vm(D, 256), vm(D, 256), vm(256, D),
            vm(4, 4, 64, Q), vm(4, 4, 64, Q), vm(4, 4, 64, Q), vm(4, 4, 64, Q),
            vm(4, 4, 64, Q), vm(4, 4, 64, Q),
            vm(3, 4, 64, Q), vm(3, 4, 64, Q), vm(4, 64, Q), vm(4, 64, Q),
            vm(3, 64, Q), vm(3, 64, Q), vm(64, Q), vm(64, Q), vm(3, 16, Q), vm(3, 16, Q),
            pltpu.VMEM((8, 2 * Q + EXT), F32), pltpu.VMEM((8, 2 * Q), F32), pltpu.VMEM((8, 2 * Q), F32),
            dma(3), dma(3), dma(3), dma(2), dma(2),
            dma(2, 3, 3), dma(2, 3, 3), dma(2, 4), dma(2, 4), dma(2, 4), dma(2, 4),
            dma(2, 3, 3), dma(2, 3, 3),
        ],
        compiler_params=pltpu.CompilerParams(
            collective_id=0, has_side_effects=True, vmem_limit_bytes=64 * 1024 * 1024
        ),
        cost_estimate=pl.CostEstimate(
            flops=6 * 1024 * D * 256, bytes_accessed=33 * 1024 * 1024, transcendentals=1024 * 256
        ),
        name="moe_and_exchange",
    )(tok, gate_weight, up_weight, down_weight)


PIECES = 8


def pick_kernel(flag, og, ou, od, rg, ru, rd, mg, mu, md, bg, bu, bd, in_sem, out_sem):
    outs, bufs = (mg, mu, md), (bg, bu, bd)

    def go(sources):
        loads, stores = [], []
        for part in range(PIECES):
            for k, (src, buf, dst) in enumerate(zip(sources, bufs, outs)):
                rows = src.shape[1] // PIECES
                at = pl.ds(part * rows, rows)
                loads.append(pltpu.make_async_copy(src.at[0, at], buf.at[at], in_sem.at[k, part]))
                stores.append(pltpu.make_async_copy(buf.at[at], dst.at[0, at], out_sem.at[k, part]))
        for cp in loads:
            cp.start()
        for load, store in zip(loads, stores):
            load.wait()
            store.start()
        for cp in stores:
            cp.wait()

    @pl.when(flag[0] == 1)
    def _():
        go((rg, ru, rd))

    @pl.when(flag[0] != 1)
    def _():
        go((og, ou, od))


def pick(flag, own, received):
    any_spec = pl.BlockSpec(memory_space=pl.ANY)
    return pl.pallas_call(
        pick_kernel,
        out_shape=tuple(jax.ShapeDtypeStruct(a.shape, a.dtype) for a in own),
        in_specs=[pl.BlockSpec(memory_space=pltpu.SMEM)] + [any_spec] * 6,
        out_specs=(any_spec,) * 3,
        scratch_shapes=[pltpu.VMEM(a.shape[1:], a.dtype) for a in own]
        + [pltpu.SemaphoreType.DMA((3, PIECES)), pltpu.SemaphoreType.DMA((3, PIECES))],
        compiler_params=pltpu.CompilerParams(vmem_limit_bytes=64 * 1024 * 1024),
        name="pick_slab",
    )(flag, *own, *received)


def on_device(tokens, routes, gates, swapped, gate_weight, up_weight, down_weight):
    mine = lax.axis_index("expert")
    named = routes[:, :, None] == jnp.arange(EXT, dtype=jnp.int32)
    by_expert = jnp.sum(jnp.where(named, gates.astype(F32)[:, :, None], 0.0), axis=1)
    wide = tokens.astype(F32)
    tok = jnp.stack(
        [jnp.concatenate([wide[:, k * 2 * Q : (k + 1) * 2 * Q], by_expert], axis=1) for k in (0, 1)]
    )
    mixed, *received = moe(tok, gate_weight, up_weight, down_weight)
    flag = lax.dynamic_slice(swapped, (lax.rem(mine, EXPERTS // 2),), (1,))
    moved = pick(flag, (gate_weight, up_weight, down_weight), received)
    return (mixed, *moved)


def solution(mesh):
    in_specs = (
        P(("expert", "dp"), None),
        P(("expert", "dp"), None),
        P(("expert", "dp"), None),
        P(),
        P("expert", None, "dp"),
        P("expert", None, "dp"),
        P("expert", "dp", None),
    )
    out_specs = (
        P(("expert", "dp"), None),
        P("expert", None, "dp"),
        P("expert", None, "dp"),
        P("expert", "dp", None),
    )
    return jax.shard_map(
        on_device, mesh=mesh, in_specs=in_specs, out_specs=out_specs, check_vma=False
    )
```

time: 799 us -> 276 us (0.35)
  waiting for transfers between devices: 626 us -> 0 us
  Pallas kernels: 0 us -> 268 us
  blocking collectives: 38.2 us -> 0 us
  other arithmetic: 36.5 us -> 2.2 us
  local copies, waits for them, and re-layouts: 34.2 us -> 3.66 us
  matrix products: 25.8 us -> 0 us
  starting transfers between devices: 21.6 us -> 0 us
  between operations: 14.8 us -> 0.67 us
    ppermute x3 -> x0, waiting for transfers between devices: 408 us -> none  [partner(): return lax.ppermute(value, axis, pairs)]
    pallas_call x0 -> x2, Pallas kernels: none -> 268 us  [the longest x1 259 us: moe(): pl.pallas_call(moe_kernel, out_shape=(jax.ShapeDtypeStruct((8, D), BF), l...]
    all_to_all x2 -> x0, waiting for transfers between devices: 181 us -> none  [the longest x1 181 us: on_device(): lax.all_to_all(partials, 'expert', split_axis=0, concat_axis=0, tiled=True)]
    all_gather x3 -> x0, blocking collectives: 38.2 us -> none  [the longest x1 13.5 us: on_device(): lax.all_gather(tokens, 'dp', axis=0, tiled=True)]
    reduce_scatter x1 -> x0, waiting for transfers between devices: 36.6 us -> none  [on_device(): lax.psum_scatter(weighted, 'dp', scatter_dimension=0, tiled=True)]
    gather x3 -> x0, local copies, waits for them, and re-layouts: 30.4 us -> none  [the longest x1 19.5 us: on_device(): picked = back.reshape(count * cap, model)[target].reshape(group, top, model)]
    dot_general x2 -> x0, matrix products: 25.8 us -> none  [the longest x1 18.9 us: expert_part(): jnp.dot(hidden, w_down, preferred_element_type=jnp.float32) * FF ** (-0.5)]
    select_n x8 -> x0, other arithmetic: 23.5 us -> none  [the longest x1 9.83 us: on_device(): jnp.where((table >= 0)[:, None], group_tok[safe], jnp.zeros((), jnp.bfloa...]
  transfers between devices with their start and end apart: 6 -> 0, of which waited for: 5 -> 0; matrix products, arithmetic and copies ran while one was open for 2% -> 0% of each run, Pallas kernels for 0% -> 0%
where the time goes in v1:
time: 276 us; the launch traced here: 275 us
  Pallas kernels  268 us (97%)
  local copies, waits for them, and re-layouts  3.66 us (1%)
    pallas_call x1, Pallas kernels, moe(): pl.pallas_call(moe_kernel, out_shape=(jax.ShapeDtypeStruct((8, D), BF), l...  259 us
    pallas_call x1, Pallas kernels, pick(): pl.pallas_call(pick_kernel, out_shape=tuple((jax.ShapeDtypeStruct(a.shape...  8.99 us

profile of v1, /device:TPU:0, one launch (start us, length us, event | category | flops | bytes accessed | tf_op | source)
XLA Modules:
  0.0 274.6 jit_solution(5220730667149915506)
XLA Ops:
  0.6 1.2 dynamic_slice.3.flag
  1.9 0.7 convert_element_type.7
  2.6 0.8 select_reduce_fusion
  3.3 0.9 fusion.2
  4.2 0.7 pad_maximum_fusion.tok
  5.0 259.1 %moe_and_exchange.1 = (bf16[8,7168]{1,0:T(8,128)(2,1)}, bf16[1,7168,256]{2,1,0:T(8,128)(2,1)}, bf16[1,7168,256]{2,1,0:T(8,128)(2,1)}, bf16[1,256,7168]{2,1,0:T(8,128)(2,1)}) custom-call(f32[2,8,3712]{2,1,0:T(8,128)} %pad_maximum_fusion.tok, bf16[1,7168,256]{2,1,0:T(8,128)(2,1)} %og.1, bf16[1,7168,256]{2,1,0:T(8,128)(2,1)} %ou.1, bf16[1,256,7168]{2,1,0:T(8,128)(2,1)} %od.1), custom_call_target="tpu_custom_call" | custom-call | flops 11274289152 | bytes 34603008 | tf_op jit(solution)/shard_map/moe_and_exchange/pallas_call | solution.py:266
  264.0 9.0 %pick_slab.1 = (bf16[1,7168,256]{2,1,0:T(8,128)(2,1)}, bf16[1,7168,256]{2,1,0:T(8,128)(2,1)}, bf16[1,256,7168]{2,1,0:T(8,128)(2,1)}) custom-call(s32[1]{0:T(128)} %dynamic_slice.3.flag, bf16[1,7168,256]{2,1,0:T(8,128)(2,1)} %og.1, bf16[1,7168,256]{2,1,0:T(8,128)(2,1)} %ou.1, bf16[1,256,7168]{2,1,0:T(8,128)(2,1)} %od.1, ...), custom_call_target="tpu_custom_call" | custom-call | tf_op jit(solution)/shard_map/pick_slab/pallas_call | solution.py:329
  273.0 1.6 copy.12
  (1 shorter events, 0.0 us)

commit v2 on v1

--- a/solution.py
+++ b/solution.py
@@ -16,15 +16,17 @@
 BF = jnp.bfloat16
 F32 = jnp.float32
 MESH = pl.DeviceIdType.MESH
+PIECES = 8
+FIRST, SECOND, THIRD, FOURTH = 1, 14, 2, 2
 
 
 def moe_kernel(
-    tok, gw, uw, dw,
+    tok, routes, gates, gw, uw, dw,
     out, rg, ru, rd,
     x0, x1, o0, o1, wg, wu, wd,
     mine0, mine1, send0, send1, core0, core1,
     r1a, r1b, s2a, s2b, r2a, r2b, s3a, s3b, r3a, r3b,
-    half_in, half_out, last_in,
+    half_to, half_in, half_out, last_in,
     wsem, swap_s, swap_r, core_s, core_r, ag_s, ag_r, fw_s, fw_r, pc_s, pc_r, rs_s, rs_r,
 ):
     e = lax.axis_index("expert")
@@ -63,13 +65,39 @@
     peers = [other] + [along[a](i) for a in "xzy" for i in (1, 2, 3)]
     for dev in peers:
         pl.semaphore_signal(barrier, inc=1, device_id=dev, device_id_type=MESH)
+
+    wide = tok[...].astype(F32)
+    named, level = routes[...], gates[...].astype(F32)
+    slot = lax.broadcasted_iota(jnp.int32, (8, EXT), 1)
+    by_expert = jnp.zeros((8, EXT), F32)
+    for k in range(8):
+        by_expert += jnp.where(named[:, k : k + 1] == slot, level[:, k : k + 1], 0.0)
+    low, high = wide[:, 0 : 2 * Q], wide[:, 2 * Q :]
+    half_to[:, 0 : 2 * Q] = jnp.where(c == 0, high, low)
+    half_to[:, 2 * Q :] = by_expert
+    own = jnp.concatenate([jnp.where(c == 0, low, high), by_expert], axis=1)
     pl.semaphore_wait(barrier, len(peers))
 
-    first = remote(tok.at[1 - c], half_in, core_s.at[0], core_r.at[0], other)
+    def slab_piece(k, part):
+        src, dst = ((gw, rg), (uw, ru), (dw, rd))[k]
+        rows = src.shape[1] // PIECES
+        at = (0, pl.ds(part * rows, rows))
+        return remote(src.at[at], dst.at[at], swap_s.at[k, part], swap_r.at[k, part], along["x"](2))
+
+    swaps = [slab_piece(k, part) for k in range(3) for part in range(PIECES)]
+    waiting = list(swaps)
+
+    def send_pieces(number):
+        for cp in waiting[:number]:
+            cp.start()
+        del waiting[:number]
+
+    send_pieces(FIRST)
+
+    first = remote(half_to, half_in, core_s.at[0], core_r.at[0], other)
     first.start()
 
     first.wait()
-    own = tok[c]
     got = half_in[...]
     block = jnp.where(
         c == 0, jnp.concatenate([own, got], axis=0), jnp.concatenate([got, own], axis=0)
@@ -97,13 +125,7 @@
     for i in (1, 2, 3):
         gather(0, 0, i, x0, (y, z, rows16), "x")
         gather(1, 0, i, x1, (y, z, rows16), "x")
-
-    swaps = [
-        remote(src.at[0], dst.at[0], swap_s.at[k], swap_r.at[k], along["x"](2))
-        for k, (src, dst) in enumerate(((gw, rg), (uw, ru), (dw, rd)))
-    ]
-    for cp in swaps:
-        cp.start()
+    send_pieces(SECOND)
 
     for i in (1, 2, 3):
         from16 = pl.ds(pl.multiple_of(shift(x, 4 - i) * 16, 16), 16)
@@ -189,6 +211,8 @@
 
     lax.fori_loop(0, 4, quarter, 0)
 
+    send_pieces(THIRD)
+
     def add_cores(a, carry):
         part_copy(0, a).wait()
         part_copy(1, a).wait()
@@ -226,6 +250,7 @@
     for i in (1, 2, 3):
         stage.append(scatter(0, 1, i, s2a.at[shift(z, i)], r2a.at[i - 1], "z"))
         stage.append(scatter(1, 1, i, s2b.at[shift(y, i)], r2b.at[i - 1], "y"))
+    send_pieces(FOURTH)
     for cp in stage:
         cp.wait_recv()
     s3a[...] = total(s2a[z], r2a).astype(BF)
@@ -235,6 +260,7 @@
         to16 = pl.ds(pl.multiple_of(shift(x, i) * 16, 16), 16)
         stage.append(scatter(0, 2, i, s3a.at[to16], r3a.at[i - 1], "x"))
         stage.append(scatter(1, 2, i, s3b.at[to16], r3b.at[i - 1], "x"))
+    send_pieces(len(waiting))
     for cp in stage:
         cp.wait_recv()
     sum_a = total(s3a[rows16, :], r3a)
@@ -257,7 +283,7 @@
         cp.wait()
 
 
-def moe(tok, gate_weight, up_weight, down_weight):
+def moe(tok, routes, gates, gate_weight, up_weight, down_weight):
     vm = lambda *shape: pltpu.VMEM(shape, BF)
     dma = lambda *shape: pltpu.SemaphoreType.DMA(shape)
     any_spec = pl.BlockSpec(memory_space=pl.ANY)
@@ -269,7 +295,7 @@
             jax.ShapeDtypeStruct((8, D), BF),
             like(gate_weight), like(up_weight), like(down_weight),
         ),
-        in_specs=[vmem_spec, any_spec, any_spec, any_spec],
+        in_specs=[vmem_spec] * 3 + [any_spec] * 3,
         out_specs=(vmem_spec, any_spec, any_spec, any_spec),
         scratch_shapes=[
             vm(4, 4, 64, W0), vm(4, 4, 64, Q), vm(4, 4, 64, W0), vm(4, 4, 64, Q),
@@ -278,8 +304,9 @@
             vm(4, 4, 64, Q), vm(4, 4, 64, Q),
             vm(3, 4, 64, Q), vm(3, 4, 64, Q), vm(4, 64, Q), vm(4, 64, Q),
             vm(3, 64, Q), vm(3, 64, Q), vm(64, Q), vm(64, Q), vm(3, 16, Q), vm(3, 16, Q),
-            pltpu.VMEM((8, 2 * Q + EXT), F32), pltpu.VMEM((8, 2 * Q), F32), pltpu.VMEM((8, 2 * Q), F32),
-            dma(3), dma(3), dma(3), dma(2), dma(2),
+            pltpu.VMEM((8, 2 * Q + EXT), F32), pltpu.VMEM((8, 2 * Q + EXT), F32),
+            pltpu.VMEM((8, 2 * Q), F32), pltpu.VMEM((8, 2 * Q), F32),
+            dma(3), dma(3, PIECES), dma(3, PIECES), dma(2), dma(2),
             dma(2, 3, 3), dma(2, 3, 3), dma(2, 4), dma(2, 4), dma(2, 4), dma(2, 4),
             dma(2, 3, 3), dma(2, 3, 3),
         ],
@@ -290,14 +317,12 @@
             flops=6 * 1024 * D * 256, bytes_accessed=33 * 1024 * 1024, transcendentals=1024 * 256
         ),
         name="moe_and_exchange",
-    )(tok, gate_weight, up_weight, down_weight)
-
-
-PIECES = 8
-
-
-def pick_kernel(flag, og, ou, od, rg, ru, rd, mg, mu, md, bg, bu, bd, in_sem, out_sem):
+    )(tok, routes, gates, gate_weight, up_weight, down_weight)
+
+
+def pick_kernel(swapped, og, ou, od, rg, ru, rd, mg, mu, md, bg, bu, bd, in_sem, out_sem):
     outs, bufs = (mg, mu, md), (bg, bu, bd)
+    flag = swapped[lax.rem(lax.axis_index("expert"), EXPERTS // 2)]
 
     def go(sources):
         loads, stores = [], []
@@ -315,16 +340,16 @@
         for cp in stores:
             cp.wait()
 
-    @pl.when(flag[0] == 1)
+    @pl.when(flag == 1)
     def _():
         go((rg, ru, rd))
 
-    @pl.when(flag[0] != 1)
+    @pl.when(flag != 1)
     def _():
         go((og, ou, od))
 
 
-def pick(flag, own, received):
+def pick(swapped, own, received):
     any_spec = pl.BlockSpec(memory_space=pl.ANY)
     return pl.pallas_call(
         pick_kernel,
@@ -335,20 +360,12 @@
         + [pltpu.SemaphoreType.DMA((3, PIECES)), pltpu.SemaphoreType.DMA((3, PIECES))],
         compiler_params=pltpu.CompilerParams(vmem_limit_bytes=64 * 1024 * 1024),
         name="pick_slab",
-    )(flag, *own, *received)
+    )(swapped, *own, *received)
 
 
 def on_device(tokens, routes, gates, swapped, gate_weight, up_weight, down_weight):
-    mine = lax.axis_index("expert")
-    named = routes[:, :, None] == jnp.arange(EXT, dtype=jnp.int32)
-    by_expert = jnp.sum(jnp.where(named, gates.astype(F32)[:, :, None], 0.0), axis=1)
-    wide = tokens.astype(F32)
-    tok = jnp.stack(
-        [jnp.concatenate([wide[:, k * 2 * Q : (k + 1) * 2 * Q], by_expert], axis=1) for k in (0, 1)]
-    )
-    mixed, *received = moe(tok, gate_weight, up_weight, down_weight)
-    flag = lax.dynamic_slice(swapped, (lax.rem(mine, EXPERTS // 2),), (1,))
-    moved = pick(flag, (gate_weight, up_weight, down_weight), received)
+    mixed, *received = moe(tokens, routes, gates, gate_weight, up_weight, down_weight)
+    moved = pick(swapped, (gate_weight, up_weight, down_weight), received)
     return (mixed, *moved)
 
 

time: 276 us -> 268 us (0.971)
  no operation moved by 1% of the time
where the time goes in v2:
time: 268 us
  Pallas kernels  266 us (99%)
    pallas_call x1, Pallas kernels, moe(): pl.pallas_call(moe_kernel, out_shape=(jax.ShapeDtypeStruct((8, D), BF), l...  257 us
    pallas_call x1, Pallas kernels, pick(): pl.pallas_call(pick_kernel, out_shape=tuple((jax.ShapeDtypeStruct(a.shape...  9.03 us

profile of v2, /device:TPU:0, one launch (start us, length us, event | category | flops | bytes accessed | tf_op | source)
XLA Modules:
  0.0 268.1 jit_solution(17943249520826923090)
XLA Ops:
  0.6 256.9 %moe_and_exchange.1 = (bf16[8,7168]{1,0:T(8,128)(2,1)}, bf16[1,7168,256]{2,1,0:T(8,128)(2,1)}, bf16[1,7168,256]{2,1,0:T(8,128)(2,1)}, bf16[1,256,7168]{2,1,0:T(8,128)(2,1)}) custom-call(bf16[8,7168]{1,0:T(8,128)(2,1)} %tok.1, s32[8,8]{1,0:T(8,128)} %routes.1, bf16[8,8]{1,0:T(8,128)(2,1)} %gates.1, bf16[1,7168,256]{2,1,0:T(8,128)(2,1)} %og.1, ...), custom_call_target="tpu_custom_call" | custom-call | flops 11274289152 | bytes 34603008 | tf_op jit(solution)/shard_map/moe_and_exchange/pallas_call | solution.py:292
  257.6 9.0 %pick_slab.1 = (bf16[1,7168,256]{2,1,0:T(8,128)(2,1)}, bf16[1,7168,256]{2,1,0:T(8,128)(2,1)}, bf16[1,256,7168]{2,1,0:T(8,128)(2,1)}) custom-call(s32[8]{0:T(128)} %swapped.1, bf16[1,7168,256]{2,1,0:T(8,128)(2,1)} %og.1, bf16[1,7168,256]{2,1,0:T(8,128)(2,1)} %ou.1, bf16[1,256,7168]{2,1,0:T(8,128)(2,1)} %od.1, bf16[1,7168,256]{2,1,0:T(8,128)(2,1)} %get-tuple-element.12.rg, ...), custom_call_target="tpu_custom_call" | custom-call | tf_op jit(solution)/shard_map/pick_slab/pallas_call | solution.py:354
  266.6 1.6 copy.12

commit v3 on v2

--- a/solution.py
+++ b/solution.py
@@ -17,17 +17,207 @@
 F32 = jnp.float32
 MESH = pl.DeviceIdType.MESH
 PIECES = 8
-FIRST, SECOND, THIRD, FOURTH = 1, 14, 2, 2
+FIRST, SECOND, THIRD, FOURTH = 1, 11, 2, 1
+
+CHUNKS = 8
+UNIT = 16
+
+ROUTES = {
+    15: ((1, 29), (0, 27), (11, 29), (10, 27), (21, 29), (20, 27), (31, 29), (30, 27)),
+    41: ((1, 22), (0, 20), (3, 7), (5, 7), (29, 13), (31, 23), (30, 20), (43, 23), (42, 13), (45, 20)),
+    51: ((1, 29), (7, 27), (11, 29), (13, 27), (33, 29), (39, 27), (43, 29), (45, 27)),
+    61: ((1, 36), (3, 20), (19, 13), (21, 36), (20, 7), (31, 36), (30, 20), (33, 36), (37, 7), (39, 13), (43, 36), (45, 20)),
+    85: ((1, 29), (3, 27), (21, 29), (23, 27), (33, 29), (35, 27), (53, 29), (55, 27)),
+    103: ((1, 36), (0, 20), (8, 6), (11, 37), (15, 13), (21, 36), (23, 20), (41, 6), (43, 37), (47, 13), (53, 36), (55, 20)),
+    107: ((1, 36), (0, 20), (11, 36), (13, 20), (29, 13), (31, 36), (30, 7), (41, 13), (43, 36), (47, 7), (53, 36), (55, 20)),
+    119: ((1, 43), (7, 13), (11, 43), (15, 13), (21, 43), (23, 13), (33, 43), (39, 13), (43, 43), (47, 13), (53, 43), (55, 13)),
+    127: ((1, 50), (6, 6), (11, 50), (14, 6), (21, 50), (22, 6), (31, 50), (30, 6), (33, 50), (39, 6), (43, 50), (47, 6), (53, 50), (55, 6)),
+    151: ((1, 36), (7, 20), (11, 36), (10, 20), (21, 36), (20, 20), (33, 36), (35, 13), (37, 7), (61, 7), (63, 36), (62, 13)),
+    153: ((1, 29), (3, 27), (29, 27), (31, 29), (33, 29), (35, 27), (61, 27), (63, 29)),
+    165: ((1, 29), (3, 27), (21, 29), (23, 27), (43, 29), (45, 27), (57, 27), (63, 29)),
+    171: ((1, 36), (0, 20), (8, 6), (11, 37), (13, 13), (29, 20), (31, 36), (41, 6), (43, 37), (45, 13), (61, 20), (63, 36)),
+    187: ((1, 43), (5, 13), (11, 43), (13, 13), (29, 13), (31, 43), (33, 43), (37, 13), (43, 43), (45, 13), (61, 13), (63, 43)),
+    195: ((1, 29), (0, 27), (11, 29), (13, 27), (51, 27), (53, 29), (63, 29), (62, 27)),
+    205: ((1, 36), (0, 20), (19, 20), (21, 36), (24, 6), (27, 13), (31, 37), (51, 20), (53, 36), (57, 6), (59, 13), (63, 37)),
+    219: ((1, 43), (5, 13), (11, 43), (10, 13), (29, 13), (31, 43), (33, 43), (35, 13), (53, 43), (52, 13), (59, 13), (63, 43)),
+    221: ((1, 43), (3, 13), (19, 13), (21, 43), (27, 13), (31, 43), (33, 43), (35, 13), (51, 13), (53, 43), (59, 13), (63, 43)),
+    231: ((1, 43), (7, 13), (11, 43), (15, 13), (21, 43), (23, 13), (41, 13), (43, 43), (49, 13), (53, 43), (57, 13), (63, 43)),
+    237: ((1, 43), (3, 13), (19, 13), (21, 43), (27, 13), (31, 43), (41, 13), (43, 43), (49, 13), (53, 43), (57, 13), (63, 43)),
+    239: ((1, 50), (0, 6), (8, 6), (11, 50), (16, 6), (21, 50), (24, 6), (31, 50), (41, 6), (43, 50), (49, 6), (53, 50), (57, 6), (63, 50)),
+    241: ((1, 36), (3, 6), (7, 14), (33, 37), (34, 7), (36, 12), (43, 36), (42, 20), (53, 36), (52, 20), (63, 36), (62, 20)),
+    247: ((1, 50), (7, 6), (11, 50), (15, 6), (21, 50), (23, 6), (33, 50), (38, 6), (43, 50), (46, 6), (53, 50), (54, 6), (63, 50), (62, 6)),
+    255: ((1, 56), (11, 56), (21, 56), (31, 56), (33, 56), (43, 56), (53, 56), (63, 56)),
+}
+SETS = sorted(ROUTES)
+SERVES = (
+    1, 0, 0, 0, 1, 0, 0, 0, 2, 2, 4, 9, 10, 13, 3, 8,
+    1, 2, 11, 5, 1, 12, 3, 8, 2, 2, 3, 7, 3, 13, 3, 8,
+    4, 14, 4, 5, 15, 6, 15, 8, 4, 7, 4, 7, 16, 16, 17, 8,
+    5, 5, 5, 5, 6, 6, 19, 8, 21, 7, 7, 7, 8, 8, 8, 8,
+    10, 14, 11, 9, 10, 12, 15, 20, 10, 9, 9, 9, 10, 13, 17, 23,
+    11, 12, 11, 18, 12, 12, 19, 20, 21, 13, 22, 22, 13, 13, 23, 23,
+    14, 14, 15, 18, 15, 16, 15, 20, 21, 16, 17, 22, 16, 16, 17, 23,
+    21, 18, 18, 18, 19, 20, 19, 20, 21, 22, 22, 22, 23, 23, 23, 23,
+)
+
+
+def legs_of(z, ring, direct, sign):
+    stops = [(0, z)]
+    if ring != z:
+        stops.append((0, ring))
+    if not direct:
+        stops.append((-sign, ring))
+    stops.append((2, z))
+    return list(zip(stops[:-1], stops[1:]))
+
+
+class Leg:
+    pass
+
+
+def layout(pairs):
+    lands, relay_rows = {}, {}
+    legs = []
+    base = {}
+    for code, units in ROUTES[pairs]:
+        parity, z, ring, direct = code // 32, code // 8 % 4, code // 2 % 4, code % 2
+        rows = units * UNIT
+        start = base.get((parity, z), 0)
+        base[parity, z] = start + rows * CHUNKS
+        before = None
+        steps = legs_of(z, ring, direct, 1 - 2 * parity)
+        for k, (a, b) in enumerate(steps):
+            leg = Leg()
+            leg.rows, leg.start, leg.before, leg.turn = rows, start, before, k
+            leg.final = k == len(steps) - 1
+            leg.move = (b[0] - a[0], b[1])
+            leg.back = (a[0] - b[0], a[1])
+            leg.sender = ((parity + a[0]) % 2, a[1])
+            leg.taker = ((parity + b[0]) % 2, b[1])
+            if not leg.final:
+                leg.land_slot = lands.get(leg.taker, 0)
+                lands[leg.taker] = leg.land_slot + 1
+                leg.relay = relay_rows.get(leg.taker, 0)
+                relay_rows[leg.taker] = leg.relay + rows * CHUNKS
+            legs.append(leg)
+            before = leg
+    return legs, max(lands.values(), default=1), max(relay_rows.values(), default=UNIT)
+
+
+def exchange_kernel(legs, src, dst, relay, end_sem, land_sem):
+    e = lax.axis_index("expert")
+    d = lax.axis_index("dp")
+    x, z = e // 4, lax.rem(e, 4)
+
+    def device(move):
+        return (lax.rem(x + move[0] + 4, 4) * 4 + move[1], d)
+
+    kinds = sorted({leg.sender for leg in legs} | {leg.taker for leg in legs})
+    barrier = pltpu.get_barrier_semaphore()
+    for kind in kinds:
+        @pl.when((lax.rem(x, 2) == kind[0]) & (z == kind[1]))
+        def _(kind=kind):
+            peers = {(leg.move[0] % 4, leg.move[1]) for leg in legs if leg.sender == kind}
+            peers |= {(leg.back[0] % 4, leg.back[1]) for leg in legs if leg.taker == kind}
+            for move in sorted(peers):
+                pl.semaphore_signal(barrier, inc=1, device_id=device(move), device_id_type=MESH)
+            pl.semaphore_wait(barrier, len(peers))
+
+    def own(leg, chunk):
+        return pl.ds(pl.multiple_of(leg.start + chunk * leg.rows, UNIT), leg.rows)
+
+    def spot(leg, chunk):
+        if leg.final:
+            return dst.at[0, own(leg, chunk)]
+        return relay.at[pl.ds(pl.multiple_of(leg.relay + chunk * leg.rows, UNIT), leg.rows)]
+
+    def copy(leg, chunk):
+        return pltpu.make_async_remote_copy(
+            src_ref=src.at[0, own(leg, chunk)] if leg.turn == 0 else spot(leg.before, chunk),
+            dst_ref=spot(leg, chunk),
+            send_sem=end_sem.at[min(leg.turn, 1)],
+            recv_sem=end_sem.at[2] if leg.final else land_sem.at[leg.land_slot, chunk],
+            device_id=device(leg.move), device_id_type=MESH,
+        )
+
+    def arrival(leg, chunk):
+        here = spot(leg, chunk)
+        return pltpu.make_async_remote_copy(
+            src_ref=here, dst_ref=here,
+            send_sem=end_sem.at[0],
+            recv_sem=land_sem.at[leg.land_slot, chunk],
+            device_id=device((2, z)), device_id_type=MESH,
+        )
+
+    def whole(ref):
+        return pltpu.make_async_remote_copy(
+            src_ref=ref, dst_ref=ref, send_sem=end_sem.at[0], recv_sem=end_sem.at[2],
+            device_id=device((2, z)), device_id_type=MESH,
+        )
+
+    for kind in kinds:
+        @pl.when((lax.rem(x, 2) == kind[0]) & (z == kind[1]))
+        def _(kind=kind):
+            out = [leg for leg in legs if leg.sender == kind]
+            late = max([leg.turn for leg in out], default=0)
+
+            def push(step, carry):
+                for turn in range(late + 1):
+                    chunk = step - turn
+
+                    @pl.when((chunk >= 0) & (chunk < CHUNKS))
+                    def _(turn=turn, chunk=chunk):
+                        for leg in out:
+                            if leg.turn == turn:
+                                if turn:
+                                    arrival(leg.before, chunk).wait_recv()
+                                copy(leg, chunk).start()
+                return carry
+
+            if out:
+                lax.fori_loop(0, CHUNKS + late, push, 0)
+            passed = sum(leg.rows for leg in out if leg.turn) * CHUNKS
+            if any(leg.final and leg.taker == kind for leg in legs):
+                whole(dst.at[0]).wait_recv()
+                whole(src.at[0]).wait_send()
+            if passed:
+                relayed = relay.at[pl.ds(0, passed)]
+                pltpu.make_async_remote_copy(
+                    src_ref=relayed, dst_ref=relayed,
+                    send_sem=end_sem.at[1], recv_sem=end_sem.at[2],
+                    device_id=device((2, z)), device_id_type=MESH,
+                ).wait_send()
+
+
+def exchange(pairs, weight):
+    any_spec = pl.BlockSpec(memory_space=pl.ANY)
+    legs, n_land, n_relay = layout(pairs)
+    return pl.pallas_call(
+        functools.partial(exchange_kernel, legs),
+        out_shape=jax.ShapeDtypeStruct(weight.shape, weight.dtype),
+        in_specs=[any_spec],
+        out_specs=any_spec,
+        scratch_shapes=[
+            pltpu.VMEM((n_relay, 256), BF),
+            pltpu.SemaphoreType.DMA((3,)),
+            pltpu.SemaphoreType.DMA((n_land, CHUNKS)),
+        ],
+        compiler_params=pltpu.CompilerParams(
+            collective_id=1 + pairs // 2, has_side_effects=True, vmem_limit_bytes=60 * 1024 * 1024
+        ),
+        cost_estimate=pl.CostEstimate(flops=0, bytes_accessed=64 * 1024 * 1024, transcendentals=0),
+        name="exchange_%d" % pairs,
+    )(weight)
 
 
 def moe_kernel(
     tok, routes, gates, gw, uw, dw,
-    out, rg, ru, rd,
+    out, rg, rd,
     x0, x1, o0, o1, wg, wu, wd,
     mine0, mine1, send0, send1, core0, core1,
     r1a, r1b, s2a, s2b, r2a, r2b, s3a, s3b, r3a, r3b,
     half_to, half_in, half_out, last_in,
-    wsem, swap_s, swap_r, core_s, core_r, ag_s, ag_r, fw_s, fw_r, pc_s, pc_r, rs_s, rs_r,
+    wsem, swap_s, swap_r, core_s, core_r, ag_s, ag_r, fw_s, fw_r, pc_s, pc_r, rs_s, rs_r, last_s, last_r, z_s, z_r,
 ):
     e = lax.axis_index("expert")
     d = lax.axis_index("dp")
@@ -79,12 +269,12 @@
     pl.semaphore_wait(barrier, len(peers))
 
     def slab_piece(k, part):
-        src, dst = ((gw, rg), (uw, ru), (dw, rd))[k]
+        src, dst = ((gw, rg), (dw, rd))[k]
         rows = src.shape[1] // PIECES
         at = (0, pl.ds(part * rows, rows))
         return remote(src.at[at], dst.at[at], swap_s.at[k, part], swap_r.at[k, part], along["x"](2))
 
-    swaps = [slab_piece(k, part) for k in range(3) for part in range(PIECES)]
+    swaps = [slab_piece(k, part) for k in range(2) for part in range(PIECES)]
     waiting = list(swaps)
 
     def send_pieces(number):
@@ -131,17 +321,35 @@
         from16 = pl.ds(pl.multiple_of(shift(x, 4 - i) * 16, 16), 16)
         landed(0, 0, i, x0, (y, z, from16))
         landed(1, 0, i, x1, (y, z, from16))
-    for i in (1, 2, 3):
+
+    def block_at(stream, first, second):
+        if stream == 0:
+            return (shift(y, second), shift(z, first))
+        return (shift(y, first), shift(z, second))
+
+    def spread(stream, j):
+        buf, axis = ((x0, "y"), (x1, "z"))[stream]
+        view = block_at(stream, j, 0)
+        for i in (1, 3, 2):
+            cp = remote(
+                buf.at[view], buf.at[view],
+                last_s.at[stream, i - 1, j], last_r.at[stream, i - 1, j], along[axis](i),
+            )
+            cp.start()
+            sent.append(cp)
+
+    for i in (1, 3, 2):
         gather(0, 1, i, x0, (y, z), "z")
         gather(1, 1, i, x1, (y, z), "y")
-    for i in (1, 2, 3):
-        landed(0, 1, i, x0, (y, shift(z, 4 - i)))
-        landed(1, 1, i, x1, (shift(y, 4 - i), z))
+    spread(0, 0)
+    spread(1, 0)
+    for i in (1, 3, 2):
+        landed(0, 1, i, x0, block_at(0, 4 - i, 0))
+        spread(0, 4 - i)
+        landed(1, 1, i, x1, block_at(1, 4 - i, 0))
+        spread(1, 4 - i)
+
     every = slice(None)
-    for i in (1, 2, 3):
-        gather(0, 2, i, x0, (y,), "y")
-        gather(1, 2, i, x1, (every, z), "z")
-
     forwards = []
 
     def forward(stream, i, view):
@@ -152,12 +360,16 @@
 
     forward(0, 0, (y,))
     forward(1, 0, (every, z))
-    for i in (1, 2, 3):
-        view0, view1 = (shift(y, 4 - i),), (every, shift(z, 4 - i))
-        landed(0, 2, i, x0, view0)
-        forward(0, i, view0)
-        landed(1, 2, i, x1, view1)
-        forward(1, i, view1)
+    for i in (1, 3, 2):
+        for stream, buf in ((0, x0), (1, x1)):
+            for j in range(4):
+                view = block_at(stream, j, 4 - i)
+                remote(
+                    buf.at[view], buf.at[view],
+                    last_s.at[stream, i - 1, j], last_r.at[stream, i - 1, j], other,
+                ).wait_recv()
+        forward(0, i, (shift(y, 4 - i),))
+        forward(1, i, (every, shift(z, 4 - i)))
     for cp in forwards:
         cp.wait()
     for cp in sent:
@@ -203,26 +415,6 @@
         src, dst = ((send0, core0), (send1, core1))[stream]
         return remote(src.at[a], dst.at[a], pc_s.at[stream, a], pc_r.at[stream, a], other)
 
-    def quarter(a, carry):
-        lax.fori_loop(2 * a, 2 * a + 2, turn, 0)
-        part_copy(0, a).start()
-        part_copy(1, a).start()
-        return carry
-
-    lax.fori_loop(0, 4, quarter, 0)
-
-    send_pieces(THIRD)
-
-    def add_cores(a, carry):
-        part_copy(0, a).wait()
-        part_copy(1, a).wait()
-        for own_ref, got_ref in ((mine0, core0), (mine1, core1)):
-            for b in range(4):
-                own_ref[a, b] = (own_ref[a, b].astype(F32) + got_ref[a, b].astype(F32)).astype(BF)
-        return carry
-
-    lax.fori_loop(0, 4, add_cores, 0)
-
     out_copies = []
 
     def scatter(stream, stage, i, src, dst, axis):
@@ -237,12 +429,54 @@
             value += got_ref[(i,) + at].astype(F32)
         return value
 
-    stage = []
-    for i in (1, 2, 3):
-        stage.append(scatter(0, 0, i, mine0.at[shift(y, i)], r1a.at[i - 1], "y"))
-        stage.append(scatter(1, 0, i, mine1.at[:, shift(z, i)], r1b.at[i - 1], "z"))
-    for cp in stage:
-        cp.wait_recv()
+    def first_y(p):
+        return remote(
+            mine0.at[shift(y, p + 1)], r1a.at[p], rs_s.at[0, 0, p], rs_r.at[0, 0, p], along["y"](p + 1)
+        )
+
+    def first_z(p, i):
+        a = shift(y, p + 1)
+        return remote(
+            mine1.at[a, shift(z, i)], r1b.at[i - 1, a], z_s.at[i - 1, p], z_r.at[i - 1, p], along["z"](i)
+        )
+
+    def quarter(q, carry):
+        @pl.when(q < 4)
+        def _():
+            a = shift(y, q + 1)
+            lax.fori_loop(2 * a, 2 * a + 2, turn, 0)
+            part_copy(0, a).start()
+            part_copy(1, a).start()
+
+        @pl.when(q > 0)
+        def _():
+            p = q - 1
+            a = shift(y, p + 1)
+            part_copy(0, a).wait()
+            part_copy(1, a).wait()
+            for own_ref, got_ref in ((mine0, core0), (mine1, core1)):
+                for b in range(4):
+                    own_ref[a, b] = (own_ref[a, b].astype(F32) + got_ref[a, b].astype(F32)).astype(BF)
+            for i in (1, 3, 2):
+                first_z(p, i).start()
+
+            @pl.when(p < 3)
+            def _():
+                first_y(p).start()
+
+        return carry
+
+    lax.fori_loop(0, 5, quarter, 0)
+    send_pieces(THIRD)
+
+    def first_landed(p, carry):
+        for i in (1, 2, 3):
+            first_z(p, i).wait()
+        return carry
+
+    lax.fori_loop(0, 4, first_landed, 0)
+    for p in range(3):
+        first_y(p).wait()
     for b in range(4):
         s2a[b] = total(mine0[y, b], r1a, (b,)).astype(BF)
         s2b[b] = total(mine1[b, z], r1b, (b,)).astype(BF)
@@ -293,10 +527,10 @@
         moe_kernel,
         out_shape=(
             jax.ShapeDtypeStruct((8, D), BF),
-            like(gate_weight), like(up_weight), like(down_weight),
+            like(gate_weight), like(down_weight),
         ),
         in_specs=[vmem_spec] * 3 + [any_spec] * 3,
-        out_specs=(vmem_spec, any_spec, any_spec, any_spec),
+        out_specs=(vmem_spec, any_spec, any_spec),
         scratch_shapes=[
             vm(4, 4, 64, W0), vm(4, 4, 64, Q), vm(4, 4, 64, W0), vm(4, 4, 64, Q),
             vm(D, 256), vm(D, 256), vm(256, D),
@@ -306,9 +540,10 @@
             vm(3, 64, Q), vm(3, 64, Q), vm(64, Q), vm(64, Q), vm(3, 16, Q), vm(3, 16, Q),
             pltpu.VMEM((8, 2 * Q + EXT), F32), pltpu.VMEM((8, 2 * Q + EXT), F32),
             pltpu.VMEM((8, 2 * Q), F32), pltpu.VMEM((8, 2 * Q), F32),
-            dma(3), dma(3, PIECES), dma(3, PIECES), dma(2), dma(2),
+            dma(3), dma(2, PIECES), dma(2, PIECES), dma(2), dma(2),
             dma(2, 3, 3), dma(2, 3, 3), dma(2, 4), dma(2, 4), dma(2, 4), dma(2, 4),
             dma(2, 3, 3), dma(2, 3, 3),
+            dma(2, 3, 4), dma(2, 3, 4), dma(3, 4), dma(3, 4),
         ],
         compiler_params=pltpu.CompilerParams(
             collective_id=0, has_side_effects=True, vmem_limit_bytes=64 * 1024 * 1024
@@ -364,8 +599,12 @@
 
 
 def on_device(tokens, routes, gates, swapped, gate_weight, up_weight, down_weight):
-    mixed, *received = moe(tokens, routes, gates, gate_weight, up_weight, down_weight)
-    moved = pick(swapped, (gate_weight, up_weight, down_weight), received)
+    mixed, got_gate, got_down = moe(tokens, routes, gates, gate_weight, up_weight, down_weight)
+    up_slab, got_gate, got_down = lax.optimization_barrier((up_weight, got_gate, got_down))
+    bits = jnp.sum(swapped[1:] * 2 ** jnp.arange(7, dtype=jnp.int32))
+    number = jnp.array(SERVES, jnp.int32)[bits]
+    got_up = lax.switch(number, [functools.partial(exchange, p) for p in SETS], up_slab)
+    moved = pick(swapped, (gate_weight, up_weight, down_weight), (got_gate, got_up, got_down))
     return (mixed, *moved)
 
 

time: 268 us -> 272 us (1.015)
    pallas_call x1, Pallas kernels: 257 us -> 179 us  [moe(): pl.pallas_call(moe_kernel, out_shape=(jax.ShapeDtypeStruct((8, D), BF), l...]
    pallas_call x0 -> x1, Pallas kernels: none -> 76 us  [exchange(): pl.pallas_call(functools.partial(exchange_kernel, legs), out_shape=jax.Sh...]
where the time goes in v3:
time: 272 us
  Pallas kernels  264 us (97%)
  between operations  3.25 us (1%)
  local copies, waits for them, and re-layouts  2.8 us (1%)
    pallas_call x1, Pallas kernels, moe(): pl.pallas_call(moe_kernel, out_shape=(jax.ShapeDtypeStruct((8, D), BF), l...  179 us
    pallas_call x1, Pallas kernels, exchange(): pl.pallas_call(functools.partial(exchange_kernel, legs), out_shape=jax.Sh...  76 us
    pallas_call x1, Pallas kernels, pick(): pl.pallas_call(pick_kernel, out_shape=tuple((jax.ShapeDtypeStruct(a.shape...  9.03 us

profile of v3, /device:TPU:0, one launch (start us, length us, event | category | flops | bytes accessed | tf_op | source)
XLA Modules:
  0.0 271.5 jit_solution(10949002041683777319)
XLA Ops:
  0.6 1.4 fusion.3
  3.9 1.2 dynamic_slice.3
  5.8 178.8 %moe_and_exchange.1 = (bf16[8,7168]{1,0:T(8,128)(2,1)}, bf16[1,7168,256]{2,1,0:T(8,128)(2,1)}, bf16[1,256,7168]{2,1,0:T(8,128)(2,1)}) custom-call(bf16[8,7168]{1,0:T(8,128)(2,1)} %tok.1, s32[8,8]{1,0:T(8,128)} %routes.1, bf16[8,8]{1,0:T(8,128)(2,1)} %gates.1, bf16[1,7168,256]{2,1,0:T(8,128)(2,1)} %og.1, bf16[1,7168,256]{2,1,0:T(8,128)(2,1)} %ou.1, ...), custom_call_target="tpu_custom_call" | custom-call | flops 11274289152 | bytes 34603008 | tf_op jit(solution)/shard_map/moe_and_exchange/pallas_call | solution.py:526
  184.6 76.3 %conditional.1 = (bf16[1,7168,256]{2,1,0:T(8,128)(2,1)}) conditional(s32[]{:T(128)} %bitcast, bf16[1,7168,256]{2,1,0:T(8,128)(2,1)} %ou.1, bf16[1,7168,256]{2,1,0:T(8,128)(2,1)} %ou.1, bf16[1,7168,256]{2,1,0:T(8,128)(2,1)} %ou.1, bf16[1,7168,256]{2,1,0:T(8,128)(2,1)} %ou.1, bf16[1,7168,256]{2,1,0:T(8,128)(2,1)} %ou.1, ...), branch_computations={%region_1.2_spmd, %region_2.3_spmd, %region_3.4_spmd, %region_4.5_... | conditional | bytes 67108872 | solution.py:606
  184.7 76.0 %exchange_127.1 = bf16[1,7168,256]{2,1,0:T(8,128)(2,1)} custom-call(bf16[1,7168,256]{2,1,0:T(8,128)(2,1)} %src.8), custom_call_target="tpu_custom_call" | custom-call | bytes 67108864 | tf_op jit(solution)/shard_map/cond/branch_8_fun/exchange_127/pallas_call | solution.py:195
  260.9 9.0 %pick_slab.1 = (bf16[1,7168,256]{2,1,0:T(8,128)(2,1)}, bf16[1,7168,256]{2,1,0:T(8,128)(2,1)}, bf16[1,256,7168]{2,1,0:T(8,128)(2,1)}) custom-call(s32[8]{0:T(128)} %swapped.1, bf16[1,7168,256]{2,1,0:T(8,128)(2,1)} %og.1, bf16[1,7168,256]{2,1,0:T(8,128)(2,1)} %ou.1, bf16[1,256,7168]{2,1,0:T(8,128)(2,1)} %od.1, bf16[1,7168,256]{2,1,0:T(8,128)(2,1)} %get-tuple-element.65.rg, ...), custom_call_target="tpu_custom_call" | custom-call | tf_op jit(solution)/shard_map/pick_slab/pallas_call | solution.py:589
  269.9 1.6 copy.37

commit v4 on v3

--- a/solution.py
+++ b/solution.py
@@ -211,8 +211,8 @@
 
 
 def moe_kernel(
-    tok, routes, gates, gw, uw, dw,
-    out, rg, rd,
+    swapped, tok, routes, gates, gw, uw, dw,
+    out, rg, rd, number,
     x0, x1, o0, o1, wg, wu, wd,
     mine0, mine1, send0, send1, core0, core1,
     r1a, r1b, s2a, s2b, r2a, r2b, s3a, s3b, r3a, r3b,
@@ -242,6 +242,14 @@
             src_ref=src, dst_ref=dst, send_sem=ss, recv_sem=rs,
             device_id=dev, device_id_type=MESH,
         )
+
+    bits = swapped[1]
+    for k in range(2, 8):
+        bits += swapped[k] * 2 ** (k - 1)
+    serving = jnp.int32(0)
+    for n, serves in enumerate(SERVES):
+        serving += jnp.where(bits == n, serves, 0)
+    number[0] = serving
 
     loads = [
         pltpu.make_async_copy(gw.at[0], wg, wsem.at[0]),
@@ -517,20 +525,22 @@
         cp.wait()
 
 
-def moe(tok, routes, gates, gate_weight, up_weight, down_weight):
+def moe(swapped, tok, routes, gates, gate_weight, up_weight, down_weight):
     vm = lambda *shape: pltpu.VMEM(shape, BF)
     dma = lambda *shape: pltpu.SemaphoreType.DMA(shape)
     any_spec = pl.BlockSpec(memory_space=pl.ANY)
     vmem_spec = pl.BlockSpec(memory_space=pltpu.VMEM)
+    smem_spec = pl.BlockSpec(memory_space=pltpu.SMEM)
     like = lambda a: jax.ShapeDtypeStruct(a.shape, a.dtype)
     return pl.pallas_call(
         moe_kernel,
         out_shape=(
             jax.ShapeDtypeStruct((8, D), BF),
             like(gate_weight), like(down_weight),
+            jax.ShapeDtypeStruct((1,), jnp.int32),
         ),
-        in_specs=[vmem_spec] * 3 + [any_spec] * 3,
-        out_specs=(vmem_spec, any_spec, any_spec),
+        in_specs=[smem_spec] + [vmem_spec] * 3 + [any_spec] * 3,
+        out_specs=(vmem_spec, any_spec, any_spec, smem_spec),
         scratch_shapes=[
             vm(4, 4, 64, W0), vm(4, 4, 64, Q), vm(4, 4, 64, W0), vm(4, 4, 64, Q),
             vm(D, 256), vm(D, 256), vm(256, D),
@@ -552,10 +562,11 @@
             flops=6 * 1024 * D * 256, bytes_accessed=33 * 1024 * 1024, transcendentals=1024 * 256
         ),
         name="moe_and_exchange",
-    )(tok, routes, gates, gate_weight, up_weight, down_weight)
-
-
-def pick_kernel(swapped, og, ou, od, rg, ru, rd, mg, mu, md, bg, bu, bd, in_sem, out_sem):
+    )(swapped, tok, routes, gates, gate_weight, up_weight, down_weight)
+
+
+def pick_kernel(swapped, mixed, og, ou, od, rg, ru, rd, out, mg, mu, md, bg, bu, bd, in_sem, out_sem):
+    out[...] = mixed[...]
     outs, bufs = (mg, mu, md), (bg, bu, bd)
     flag = swapped[lax.rem(lax.axis_index("expert"), EXPERTS // 2)]
 
@@ -584,28 +595,31 @@
         go((og, ou, od))
 
 
-def pick(swapped, own, received):
+def pick(swapped, mixed, own, received):
     any_spec = pl.BlockSpec(memory_space=pl.ANY)
+    vmem_spec = pl.BlockSpec(memory_space=pltpu.VMEM)
     return pl.pallas_call(
         pick_kernel,
-        out_shape=tuple(jax.ShapeDtypeStruct(a.shape, a.dtype) for a in own),
-        in_specs=[pl.BlockSpec(memory_space=pltpu.SMEM)] + [any_spec] * 6,
-        out_specs=(any_spec,) * 3,
+        out_shape=tuple(jax.ShapeDtypeStruct(a.shape, a.dtype) for a in (mixed, *own)),
+        in_specs=[pl.BlockSpec(memory_space=pltpu.SMEM), vmem_spec] + [any_spec] * 6,
+        out_specs=(vmem_spec,) + (any_spec,) * 3,
         scratch_shapes=[pltpu.VMEM(a.shape[1:], a.dtype) for a in own]
         + [pltpu.SemaphoreType.DMA((3, PIECES)), pltpu.SemaphoreType.DMA((3, PIECES))],
         compiler_params=pltpu.CompilerParams(vmem_limit_bytes=64 * 1024 * 1024),
         name="pick_slab",
-    )(swapped, *own, *received)
+    )(swapped, mixed, *own, *received)
 
 
 def on_device(tokens, routes, gates, swapped, gate_weight, up_weight, down_weight):
-    mixed, got_gate, got_down = moe(tokens, routes, gates, gate_weight, up_weight, down_weight)
-    up_slab, got_gate, got_down = lax.optimization_barrier((up_weight, got_gate, got_down))
-    bits = jnp.sum(swapped[1:] * 2 ** jnp.arange(7, dtype=jnp.int32))
-    number = jnp.array(SERVES, jnp.int32)[bits]
-    got_up = lax.switch(number, [functools.partial(exchange, p) for p in SETS], up_slab)
-    moved = pick(swapped, (gate_weight, up_weight, down_weight), (got_gate, got_up, got_down))
-    return (mixed, *moved)
+    mixed, got_gate, got_down, number = moe(
+        swapped, tokens, routes, gates, gate_weight, up_weight, down_weight
+    )
+    got_up = lax.switch(
+        number[0], [functools.partial(exchange, p) for p in SETS], up_weight
+    )
+    return pick(
+        swapped, mixed, (gate_weight, up_weight, down_weight), (got_gate, got_up, got_down)
+    )
 
 
 def solution(mesh):

time: 272 us -> 248 us (0.912)
  Pallas kernels: 264 us -> 246 us
  local copies, waits for them, and re-layouts: 2.8 us -> 0 us
    pallas_call x1, Pallas kernels: 76 us -> 57.1 us  [exchange(): pl.pallas_call(functools.partial(exchange_kernel, legs), out_shape=jax.Sh...]
where the time goes in v4:
time: 248 us
  Pallas kernels  246 us (99%)
    pallas_call x1, Pallas kernels, moe(): pl.pallas_call(moe_kernel, out_shape=(jax.ShapeDtypeStruct((8, D), BF), l...  179 us
    pallas_call x1, Pallas kernels, exchange(): pl.pallas_call(functools.partial(exchange_kernel, legs), out_shape=jax.Sh...  57.1 us
    pallas_call x1, Pallas kernels, pick(): pl.pallas_call(pick_kernel, out_shape=tuple((jax.ShapeDtypeStruct(a.shape...  9.92 us

profile of v4, /device:TPU:0, one launch (start us, length us, event | category | flops | bytes accessed | tf_op | source)
XLA Modules:
  0.0 247.6 jit_solution(2184957073868078838)
XLA Ops:
  0.6 179.0 %moe_and_exchange.1 = (bf16[8,7168]{1,0:T(8,128)(2,1)}, bf16[1,7168,256]{2,1,0:T(8,128)(2,1)}, bf16[1,256,7168]{2,1,0:T(8,128)(2,1)}, s32[1]{0:T(128)}) custom-call(s32[8]{0:T(128)} %swapped.3, bf16[8,7168]{1,0:T(8,128)(2,1)} %tok.1, s32[8,8]{1,0:T(8,128)} %routes.1, bf16[8,8]{1,0:T(8,128)(2,1)} %gates.1, bf16[1,7168,256]{2,1,0:T(8,128)(2,1)} %og.1, ...), custom_call_target="tpu_custom_call" | custom-call | flops 11274289152 | bytes 34603008 | tf_op jit(solution)/shard_map/moe_and_exchange/pallas_call | solution.py:535
  180.2 57.3 %conditional.1 = (bf16[1,7168,256]{2,1,0:T(8,128)(2,1)}) conditional(s32[]{:T(128)} %bitcast, bf16[1,7168,256]{2,1,0:T(8,128)(2,1)} %ou.1, bf16[1,7168,256]{2,1,0:T(8,128)(2,1)} %ou.1, bf16[1,7168,256]{2,1,0:T(8,128)(2,1)} %ou.1, bf16[1,7168,256]{2,1,0:T(8,128)(2,1)} %ou.1, bf16[1,7168,256]{2,1,0:T(8,128)(2,1)} %ou.1, ...), branch_computations={%region_0.0_spmd, %region_1.0_spmd, %region_2.0_spmd, %region_3.0_... | conditional | bytes 67108872 | solution.py:617
  180.5 57.1 %exchange_241.1 = bf16[1,7168,256]{2,1,0:T(8,128)(2,1)} custom-call(bf16[1,7168,256]{2,1,0:T(8,128)(2,1)} %src.21), custom_call_target="tpu_custom_call" | custom-call | bytes 67108864 | tf_op jit(solution)/shard_map/cond/branch_21_fun/exchange_241/pallas_call | solution.py:195
  237.6 9.9 %pick_slab.1 = (bf16[8,7168]{1,0:T(8,128)(2,1)}, bf16[1,7168,256]{2,1,0:T(8,128)(2,1)}, bf16[1,7168,256]{2,1,0:T(8,128)(2,1)}, bf16[1,256,7168]{2,1,0:T(8,128)(2,1)}) custom-call(s32[8]{0:T(128)} %swapped.3, bf16[8,7168]{1,0:T(8,128)(2,1)} %get-tuple-element.57.mixed, bf16[1,7168,256]{2,1,0:T(8,128)(2,1)} %og.1, bf16[1,7168,256]{2,1,0:T(8,128)(2,1)} %ou.1, ...), custom_call_target="tpu_custom_call" | custom-call | tf_op jit(solution)/shard_map/pick_slab/pallas_call | solution.py:601
